TPU v7x, 32 devices: a whole 2x2x4 slice. The times are simulated.
32 devices in a mesh: space: 8 (over z, y), tm: 4 (over x, core).
Axes of the slice: x: 2, y: 2, z: 4, core: 2. Of those that a mesh axis runs over, the one named last changes fastest.
Arguments:
- initial: float32 [3, 32, 128, 128], P(None, 'space'), may hold values from -6 to 6
- guess: float32 [8, 3, 32, 128, 128], P('tm', None, 'space'), may hold values from -6 to 6
- coarse_map: float32 [3, 3, 32, 128, 128], P(None, None, 'space'), may hold values from -0.12 to 0.99
- sites: int32 [32, 128, 128], P('space'), may hold values from 0 to 127
- mobility: float32 [128], replicated, may hold values from 0.01 to 0.08
Outputs:
- corrected: float32 [8, 3, 32, 128, 128], P('tm', None, 'space')
All inputs are finite; a program needn't handle non-finite values.
Results may differ from a plain program's by a relative error of at most 0.00002.
Values sent between devices are 32-bit elements; how exact they have to be, the bound alone decides.
A program may use at most 128 MiB of HBM per device.

v0:
```python
import functools

import jax
import jax.numpy as jnp
from jax import lax
from jax.experimental import pallas as pl
from jax.experimental.pallas import tpu as pltpu
from jax.sharding import PartitionSpec as P

M = 16
PAD = 8
ROWS = 32
MESH = pl.DeviceIdType.MESH

diffusion_number = 0.15
heat_release = 0.5
hardening = 0.02
saturation = 2.0


def kernel(
    spaces, blocks,
    initial, guess, coarse, sites, mobility, out,
    heat_a, heat_b, heat_c, dens, prog, mobile, own_mobile,
    relaxed, relaxed_out, fine, arriving, maps,
    start_send, start_recv, local_sem, mob_send, mob_recv,
    halo_send, halo_recv, edge_send, edge_recv,
    relaxed_send, relaxed_recv, back_send, back_recv, chain_send, chain_recv, map_sem,
):
    depth = sites.shape[0]
    ny, nx = sites.shape[1], sites.shape[2]
    s, t = lax.axis_index("space"), lax.axis_index("tm")
    half = lax.rem(s, 2)
    first, last = t == 0, t == blocks - 1
    later = jnp.logical_not(first)
    thick = jnp.where(first, depth, 2 * depth)
    stride = jnp.where(first, 1, 2)
    offset = jnp.where(first, 0, half * depth)
    other = 1 - half
    base = s - half
    partner = base + other
    has_low, has_high = s >= stride, s < spaces - stride
    rows = pl.ds(PAD, ny)

    barrier = pltpu.get_barrier_semaphore()

    def place(space, tm):
        return {"space": space, "tm": tm}

    zero_rows = jnp.zeros((PAD, nx), jnp.float32)
    for heat in (heat_a, heat_b, heat_c):
        for layer in range(2 * depth + 4):
            heat[layer, pl.ds(0, PAD), :] = zero_rows
            heat[layer, pl.ds(PAD + ny, PAD), :] = zero_rows
        for layer in (0, 1, thick + 2, thick + 3):
            heat[layer, rows, :] = jnp.zeros((ny, nx), jnp.float32)

    friends = [
        (later, partner, t),
        (t > 0, base, t - 1), (t > 0, base + 1, t - 1),
        (t < blocks - 1, base, t + 1), (t < blocks - 1, base + 1, t + 1),
        (has_low, s - stride, t), (has_high, s + stride, t),
    ]
    count = 0
    for there, space, tm in friends:
        @pl.when(there)
        def _(space=space, tm=tm):
            pl.semaphore_signal(barrier, 1, device_id=place(space, tm), device_id_type=MESH)
        count = count + there.astype(jnp.int32)
    pl.semaphore_wait(barrier, count)


    def landing(field, where):
        start = where * depth
        if field == 0:
            return heat_a.at[pl.ds(start + 2, depth), rows, :]
        return (dens, prog)[field - 1].at[pl.ds(start + 1, depth)]

    def start_copy(source, chain, field, tm):
        return pltpu.make_async_remote_copy(
            source, landing(field, half), start_send.at[chain, field], start_recv.at[half, field],
            device_id=place(base + chain, tm), device_id_type=MESH)

    def local_copy(field):
        return pltpu.make_async_copy(initial.at[field], landing(field, 0), local_sem.at[field])

    map_copy = pltpu.make_async_copy(coarse, maps, map_sem)

    @pl.when(first)
    def _():
        for field in range(3):
            local_copy(field).start()

    @pl.when(jnp.logical_not(last))
    def _():
        for field in range(3):
            for chain in range(2):
                start_copy(guess.at[chain, field], chain, field, t + 1).start()

    table = jnp.broadcast_to(mobility[...], (8, nx))

    def look_up(layer, carry):
        for row in range(0, ny, 8):
            index = sites[layer, pl.ds(row, 8), :]
            found = jnp.take_along_axis(table, index, axis=1, mode="promise_in_bounds")
            own_mobile[layer, pl.ds(row, 8), :] = found
            mobile[layer + 1 + offset, pl.ds(row, 8), :] = found
        return carry

    lax.fori_loop(0, depth, look_up, 0)
    mobile_copy = pltpu.make_async_remote_copy(
        own_mobile, mobile.at[pl.ds(1 + half * depth, depth)], mob_send, mob_recv,
        device_id=place(partner, t), device_id_type=MESH)

    @pl.when(later)
    def _():
        mobile_copy.start()

    map_copy.start()

    @pl.when(first)
    def _():
        for field in range(3):
            local_copy(field).wait()

    @pl.when(later)
    def _():
        for field in range(3):
            for source in range(2):
                pltpu.make_async_remote_copy(
                    guess.at[0, field], landing(field, source), start_send.at[0, field], start_recv.at[source, field],
                    device_id=place(partner, t), device_id_type=MESH).wait_recv()
        mobile_copy.wait()

    def halo(heat, parity, side, far):
        source, target, space = (
            (2 + far, thick + 2 + far, s - stride), (thick + 1 - far, 1 - far, s + stride))[side]
        return pltpu.make_async_remote_copy(
            heat.at[source, rows, :], heat.at[target, rows, :],
            halo_send.at[parity, side, far], halo_recv.at[parity, side, far],
            device_id=place(space, t), device_id_type=MESH)

    def send_halo(heat, parity, side, far, go):
        @pl.when(jnp.logical_and((has_low, has_high)[side], go))
        def _():
            halo(heat, parity, side, far).start()

    def wait_halo(heat, parity, side, far):
        @pl.when((has_low, has_high)[side])
        def _():
            halo(heat, parity, side, far).wait_send()
            halo(heat, parity, 1 - side, far).wait_recv()

    for far in range(2):
        for side in range(2):
            send_halo(heat_a, 0, side, far, True)
    edges = (dens, prog, mobile)

    def edge(number, side):
        ref = edges[number]
        source, target, space = ((1, thick + 1, s - stride), (thick, 0, s + stride))[side]
        return pltpu.make_async_remote_copy(
            ref.at[source], ref.at[target], edge_send.at[number, side], edge_recv.at[number, side],
            device_id=place(space, t), device_id_type=MESH)

    @pl.when(has_low)
    def _():
        for number in range(3):
            edge(number, 0).start()

    @pl.when(has_high)
    def _():
        for number in range(3):
            edge(number, 1).start()

    @pl.when(has_low)
    def _():
        for number in range(3):
            edge(number, 0).wait_send()
            edge(number, 1).wait_recv()

    @pl.when(has_high)
    def _():
        for number in range(3):
            edge(number, 1).wait_send()
            edge(number, 0).wait_recv()

    lane = lax.broadcasted_iota(jnp.int32, (ROWS, nx), 1)
    not_first, not_last = lane > 0, lane < nx - 1

    def update(source, target, layer):
        for row in range(0, ny, ROWS):
            here = pl.ds(row, ROWS)
            center = source[layer, pl.ds(PAD + row, ROWS), :]
            density = dens[layer - 1, here, :]
            progress = prog[layer - 1, here, :]
            square = density * density
            driving = square * pl.reciprocal(1.0 + square)
            growth = mobile[layer - 1, here, :] * (1.0 + 0.5 * jnp.tanh(center)) * driving
            growth = growth * (1.0 - jnp.tanh(progress))
            if target is not None:
                around = source[layer - 1, pl.ds(PAD + row, ROWS), :] + source[layer + 1, pl.ds(PAD + row, ROWS), :]
                around = around + (source[layer, pl.ds(PAD + row - 1, ROWS), :] + source[layer, pl.ds(PAD + row + 1, ROWS), :])
                left = jnp.where(not_first, pltpu.roll(center, 1, 1), 0.0)
                right = jnp.where(not_last, pltpu.roll(center, nx - 1, 1), 0.0)
                around = around + (left + right)
                target[layer, pl.ds(PAD + row, ROWS), :] = (
                    (1.0 - 6.0 * diffusion_number) * center + diffusion_number * around + heat_release * growth)
            dens[layer - 1, here, :] = density * ((1.0 - hardening) - growth) + hardening * saturation
            prog[layer - 1, here, :] = progress + growth

    def sweep(source, target, low, high):
        def body(layer, carry):
            update(source, target, layer)
            return carry
        lax.fori_loop(low, high, body, 0)

    def cycle(source, middle, target, parity, go):
        sweep(source, middle, 3, thick + 1)
        wait_halo(source, parity, 0, 0)
        update(source, middle, 2)
        update(middle, target, 3)
        send_halo(target, 1 - parity, 0, 1, go)
        wait_halo(source, parity, 1, 0)
        update(source, middle, thick + 1)
        update(middle, target, thick)
        send_halo(target, 1 - parity, 1, 1, go)
        wait_halo(source, parity, 0, 1)
        sweep(source, middle, 1, jnp.where(has_low, 2, 1))
        update(middle, target, 2)
        send_halo(target, 1 - parity, 0, 0, go)
        wait_halo(source, parity, 1, 1)
        sweep(source, middle, thick + 2, jnp.where(has_high, thick + 3, thick + 2))
        update(middle, target, thick + 1)
        send_halo(target, 1 - parity, 1, 0, go)
        sweep(middle, target, 4, thick)
        sweep(middle, None, jnp.where(has_low, 1, 2), 2)
        sweep(middle, None, thick + 2, jnp.where(has_high, thick + 3, thick + 2))

    total = 2 * M // 4

    def four_steps(index, carry):
        cycle(heat_a, heat_b, heat_c, 0, True)
        cycle(heat_c, heat_b, heat_a, 1, index < total - 1)
        return carry

    lax.fori_loop(0, total // 2, four_steps, 0)

    def state(field, layer):
        if field == 0:
            return heat_a[layer + 2, rows, :]
        return (dens, prog)[field - 1][layer + 1]

    def keep(layer, carry):
        for field in range(3):
            relaxed[half, field, layer] = state(field, offset + layer)

        @pl.when(later)
        def _():
            for field in range(3):
                relaxed_out[field, layer] = state(field, other * depth + layer)
        return carry

    lax.fori_loop(0, depth, keep, 0)

    def relaxed_copy(chain):
        return pltpu.make_async_remote_copy(
            relaxed_out, relaxed.at[chain], relaxed_send, relaxed_recv,
            device_id=place(partner, t), device_id_type=MESH)

    def fine_copy(field, chain, where, layer):
        start = where * depth + layer
        source = heat_a.at[start + 2, rows, :] if field == 0 else (dens, prog)[field - 1].at[start + 1]
        return pltpu.make_async_remote_copy(
            source, fine.at[chain, field, layer], back_send.at[field, layer], back_recv.at[field, layer],
            device_id=place(partner, t), device_id_type=MESH)

    @pl.when(later)
    def _():
        relaxed_copy(half).start()

    lax.fori_loop(total // 2, total, four_steps, 0)

    @pl.when(later)
    def _():
        for layer in range(depth):
            for field in range(3):
                fine_copy(field, half, other, layer).start()

    def keep_fine(layer, carry):
        for field in range(3):
            fine[half, field, layer] = state(field, offset + layer)
        return carry

    lax.fori_loop(0, depth, keep_fine, 0)
    map_copy.wait()

    @pl.when(jnp.logical_not(last))
    def _():
        for field in range(3):
            for chain in range(2):
                start_copy(guess.at[chain, field], chain, field, t + 1).wait_send()

    @pl.when(later)
    def _():
        relaxed_copy(half).wait_send()
        relaxed_copy(other).wait_recv()

    def chain_copy(layer, tm):
        return pltpu.make_async_remote_copy(
            out.at[1, :, layer], arriving.at[:, layer], chain_send.at[layer], chain_recv.at[layer],
            device_id=place(s, tm), device_id_type=MESH)

    def link(layer, carry):
        @pl.when(first)
        def _():
            for field in range(3):
                out[0, field, layer] = relaxed[half, field, layer]
                out[1, field, layer] = fine[half, field, layer]

        @pl.when(later)
        def _():
            for field in range(3):
                fine_copy(field, other, half, layer).wait_recv()
            chain_copy(layer, t).wait_recv()
            for row in range(0, ny, ROWS):
                here = pl.ds(row, ROWS)
                value = [arriving[field, layer, here, :] for field in range(3)]
                for slot in range(2):
                    change = [value[field] - relaxed[slot, field, layer, here, :] for field in range(3)]
                    value = [
                        fine[slot, r, layer, here, :]
                        + (maps[r, 0, layer, here, :] * change[0] + maps[r, 1, layer, here, :] * change[1]
                           + maps[r, 2, layer, here, :] * change[2])
                        for r in range(3)
                    ]
                    for field in range(3):
                        out[slot, field, layer, here, :] = value[field]

        @pl.when(jnp.logical_not(last))
        def _():
            chain_copy(layer, t + 1).start()
        return carry

    lax.fori_loop(0, depth, link, 0)

    @pl.when(jnp.logical_not(last))
    def _():
        for layer in range(depth):
            chain_copy(layer, t + 1).wait_send()

    @pl.when(later)
    def _():
        for layer in range(depth):
            for field in range(3):
                fine_copy(field, half, other, layer).wait_send()


def shards(spaces, blocks, initial, guess, coarse_map, sites, mobility):
    depth, ny, nx = sites.shape
    thick = 2 * depth
    heat = pltpu.VMEM((thick + 4, ny + 2 * PAD, nx), jnp.float32)
    wide = pltpu.VMEM((thick + 2, ny, nx), jnp.float32)
    both = pltpu.VMEM((2, 3, depth, ny, nx), jnp.float32)
    one = pltpu.VMEM((3, depth, ny, nx), jnp.float32)
    dma = pltpu.SemaphoreType.DMA
    vmem = pl.BlockSpec(memory_space=pltpu.VMEM)
    hbm = pl.BlockSpec(memory_space=pl.ANY)
    return pl.pallas_call(
        functools.partial(kernel, spaces, blocks),
        out_shape=jax.ShapeDtypeStruct(guess.shape, jnp.float32),
        in_specs=[hbm, hbm, hbm, vmem, vmem],
        out_specs=vmem,
        scratch_shapes=[
            heat, heat, heat, wide, wide, wide, pltpu.VMEM((depth, ny, nx), jnp.float32),
            both, one, both, one, pltpu.VMEM(coarse_map.shape, jnp.float32),
            dma((2, 3)), dma((2, 3)), dma((3,)), dma, dma,
            dma((2, 2, 2)), dma((2, 2, 2)), dma((3, 2)), dma((3, 2)),
            dma, dma, dma((3, depth)), dma((3, depth)), dma((depth,)), dma((depth,)), dma,
        ],
        compiler_params=pltpu.CompilerParams(
            collective_id=0, has_side_effects=True, vmem_limit_bytes=60 * 1024 * 1024),
    )(initial, guess, coarse_map, sites, mobility.reshape(1, -1))


def solution(mesh):
    placed = (
        P(None, "space", None, None),
        P("tm", None, "space", None, None),
        P(None, None, "space", None, None),
        P("space", None, None),
        P(),
    )
    return jax.shard_map(
        functools.partial(shards, mesh.shape["space"], mesh.shape["tm"]),
        mesh=mesh,
        in_specs=placed,
        out_specs=P("tm", None, "space", None, None),
        check_vma=False,
    )
```

profile of v0, /device:TPU:15, one launch (start us, length us, event | category | flops | bytes accessed | tf_op | source)
XLA Modules:
  0.0 125.5 jit_solution(9654683660249608667)
XLA Ops:
  0.0 122.8 %shard_map.55 = f32[2,3,4,128,128]{4,3,2,1,0:T(8,128)} custom-call(f32[3,4,128,128]{3,2,1,0:T(8,128)} %initial.1, f32[2,3,4,128,128]{4,3,2,1,0:T(8,128)} %guess.1, f32[3,3,4,128,128]{4,3,2,1,0:T(8,128)} %coarse.1, s32[4,128,128]{2,1,0:T(8,128)} %sites.1, f32[1,128]{1,0:T(1,128)} %bitcast.1), custom_call_target="tpu_custom_call" | custom-call | tf_op jit(solution)/shard_map/pallas_call | solution.py:369
  122.8 2.7 %copy.7 = f32[2,3,4,128,128]{4,3,2,1,0:T(8,128)} copy(f32[2,3,4,128,128]{4,3,2,1,0:T(8,128)} %shard_map.55) | data formatting | bytes 3145728
where the time goes:
time: 127 us; the launch traced here: 126 us
  Pallas kernels  123 us (97%)
  local copies, waits for them, and re-layouts  2.7 us (2%)
    pallas_call x1, Pallas kernels, shards(): pl.pallas_call(functools.partial(kernel, spaces, blocks), out_shape=jax.S...  123 us
    unnamed x1, local copies, waits for them, and re-layouts  2.7 us

commit v1 on v0

--- a/solution.py
+++ b/solution.py
@@ -10,6 +10,8 @@
 M = 16
 PAD = 8
 ROWS = 32
+EDGE = 2
+CHUNKS = 2
 MESH = pl.DeviceIdType.MESH
 
 diffusion_number = 0.15
@@ -23,7 +25,7 @@
     initial, guess, coarse, sites, mobility, out,
     heat_a, heat_b, heat_c, dens, prog, mobile, own_mobile,
     relaxed, relaxed_out, fine, arriving, maps,
-    start_send, start_recv, local_sem, mob_send, mob_recv,
+    start_send, start_recv, local_sem, first_send, mob_send, mob_recv,
     halo_send, halo_recv, edge_send, edge_recv,
     relaxed_send, relaxed_recv, back_send, back_recv, chain_send, chain_recv, map_sem,
 ):
@@ -33,9 +35,8 @@
     half = lax.rem(s, 2)
     first, last = t == 0, t == blocks - 1
     later = jnp.logical_not(first)
-    thick = jnp.where(first, depth, 2 * depth)
-    stride = jnp.where(first, 1, 2)
-    offset = jnp.where(first, 0, half * depth)
+    thick, stride = 2 * depth, 2
+    offset = half * depth
     other = 1 - half
     base = s - half
     partner = base + other
@@ -56,7 +57,7 @@
             heat[layer, rows, :] = jnp.zeros((ny, nx), jnp.float32)
 
     friends = [
-        (later, partner, t),
+        (t >= 0, partner, t),
         (t > 0, base, t - 1), (t > 0, base + 1, t - 1),
         (t < blocks - 1, base, t + 1), (t < blocks - 1, base + 1, t + 1),
         (has_low, s - stride, t), (has_high, s + stride, t),
@@ -67,22 +68,33 @@
         def _(space=space, tm=tm):
             pl.semaphore_signal(barrier, 1, device_id=place(space, tm), device_id_type=MESH)
         count = count + there.astype(jnp.int32)
-    pl.semaphore_wait(barrier, count)
-
-
-    def landing(field, where):
-        start = where * depth
+    def piece_of(source, piece):
+        if piece == 0:
+            return source * (depth - EDGE), EDGE
+        return (1 - source) * EDGE, depth - EDGE
+
+    def landing(field, where, low, layers):
+        start = where * depth + low
         if field == 0:
-            return heat_a.at[pl.ds(start + 2, depth), rows, :]
-        return (dens, prog)[field - 1].at[pl.ds(start + 1, depth)]
-
-    def start_copy(source, chain, field, tm):
-        return pltpu.make_async_remote_copy(
-            source, landing(field, half), start_send.at[chain, field], start_recv.at[half, field],
+            return heat_a.at[pl.ds(start + 2, layers), rows, :]
+        return (dens, prog)[field - 1].at[pl.ds(start + 1, layers)]
+
+    def start_copy(source, chain, field, piece, tm):
+        low, layers = piece_of(source, piece)
+        return pltpu.make_async_remote_copy(
+            guess.at[chain, field, pl.ds(low, layers)], landing(field, source, low, layers),
+            start_send.at[chain, field, piece], start_recv.at[source, field, piece],
             device_id=place(base + chain, tm), device_id_type=MESH)
 
     def local_copy(field):
-        return pltpu.make_async_copy(initial.at[field], landing(field, 0), local_sem.at[field])
+        return pltpu.make_async_copy(initial.at[field], landing(field, half, 0, depth), local_sem.at[field])
+
+    def first_copy(source, field, piece):
+        low, layers = piece_of(source, piece)
+        return pltpu.make_async_remote_copy(
+            initial.at[field, pl.ds(low, layers)], landing(field, source, low, layers),
+            first_send.at[field, piece], start_recv.at[source, field, piece],
+            device_id=place(partner, t), device_id_type=MESH)
 
     map_copy = pltpu.make_async_copy(coarse, maps, map_sem)
 
@@ -90,12 +102,6 @@
     def _():
         for field in range(3):
             local_copy(field).start()
-
-    @pl.when(jnp.logical_not(last))
-    def _():
-        for field in range(3):
-            for chain in range(2):
-                start_copy(guess.at[chain, field], chain, field, t + 1).start()
 
     table = jnp.broadcast_to(mobility[...], (8, nx))
 
@@ -111,49 +117,86 @@
     mobile_copy = pltpu.make_async_remote_copy(
         own_mobile, mobile.at[pl.ds(1 + half * depth, depth)], mob_send, mob_recv,
         device_id=place(partner, t), device_id_type=MESH)
-
-    @pl.when(later)
+    pl.semaphore_wait(barrier, count)
+
+    odd = lax.rem(t, 2) == 1
+    deferred = jnp.logical_and(later, jnp.logical_not(odd))
+    mobile_late = jnp.logical_or(first, jnp.logical_and(odd, t > 2))
+
+    def send_start(go):
+        @pl.when(jnp.logical_and(jnp.logical_not(last), go))
+        def _():
+            for piece in range(2):
+                for field in range(3):
+                    for chain in range(2):
+                        start_copy(half, chain, field, piece, t + 1).start()
+
+    def wait_sent(go):
+        @pl.when(jnp.logical_and(jnp.logical_not(last), go))
+        def _():
+            for field in range(3):
+                for chain in range(2):
+                    for piece in range(2):
+                        start_copy(half, chain, field, piece, t + 1).wait_send()
+
+    def wait_start(piece):
+        for field in range(3):
+            start_copy(other, 0, field, piece, t).wait_recv()
+
+        @pl.when(later)
+        def _():
+            for field in range(3):
+                start_copy(half, 0, field, piece, t).wait_recv()
+
+    send_start(jnp.logical_not(deferred))
+
+    @pl.when(jnp.logical_not(mobile_late))
     def _():
         mobile_copy.start()
 
     map_copy.start()
+    wait_sent(first)
 
     @pl.when(first)
     def _():
+        for piece in range(2):
+            for field in range(3):
+                first_copy(half, field, piece).start()
         for field in range(3):
             local_copy(field).wait()
 
-    @pl.when(later)
-    def _():
-        for field in range(3):
-            for source in range(2):
-                pltpu.make_async_remote_copy(
-                    guess.at[0, field], landing(field, source), start_send.at[0, field], start_recv.at[source, field],
-                    device_id=place(partner, t), device_id_type=MESH).wait_recv()
-        mobile_copy.wait()
-
-    def halo(heat, parity, side, far):
+    wait_start(0)
+
+    @pl.when(mobile_late)
+    def _():
+        mobile_copy.start()
+
+    part = ny // CHUNKS
+
+    def halo(heat, parity, side, far, chunk):
         source, target, space = (
             (2 + far, thick + 2 + far, s - stride), (thick + 1 - far, 1 - far, s + stride))[side]
-        return pltpu.make_async_remote_copy(
-            heat.at[source, rows, :], heat.at[target, rows, :],
-            halo_send.at[parity, side, far], halo_recv.at[parity, side, far],
+        some = pl.ds(PAD + chunk * part, part)
+        return pltpu.make_async_remote_copy(
+            heat.at[source, some, :], heat.at[target, some, :],
+            halo_send.at[parity, side, far, chunk], halo_recv.at[parity, side, far, chunk],
             device_id=place(space, t), device_id_type=MESH)
 
-    def send_halo(heat, parity, side, far, go):
+    def send_halo(heat, parity, side, far, chunk, go):
         @pl.when(jnp.logical_and((has_low, has_high)[side], go))
         def _():
-            halo(heat, parity, side, far).start()
-
-    def wait_halo(heat, parity, side, far):
+            halo(heat, parity, side, far, chunk).start()
+
+    def wait_halo(heat, parity, side, far, chunk):
         @pl.when((has_low, has_high)[side])
         def _():
-            halo(heat, parity, side, far).wait_send()
-            halo(heat, parity, 1 - side, far).wait_recv()
+            halo(heat, parity, side, far, chunk).wait_send()
+            halo(heat, parity, 1 - side, far, chunk).wait_recv()
 
     for far in range(2):
         for side in range(2):
-            send_halo(heat_a, 0, side, far, True)
+            for chunk in range(CHUNKS):
+                send_halo(heat_a, 0, side, far, chunk, True)
     edges = (dens, prog, mobile)
 
     def edge(number, side):
@@ -163,32 +206,34 @@
             ref.at[source], ref.at[target], edge_send.at[number, side], edge_recv.at[number, side],
             device_id=place(space, t), device_id_type=MESH)
 
-    @pl.when(has_low)
-    def _():
-        for number in range(3):
-            edge(number, 0).start()
-
-    @pl.when(has_high)
-    def _():
-        for number in range(3):
-            edge(number, 1).start()
-
-    @pl.when(has_low)
-    def _():
-        for number in range(3):
-            edge(number, 0).wait_send()
-            edge(number, 1).wait_recv()
-
-    @pl.when(has_high)
-    def _():
-        for number in range(3):
-            edge(number, 1).wait_send()
-            edge(number, 0).wait_recv()
+    def send_edges(numbers):
+        for side in range(2):
+            @pl.when((has_low, has_high)[side])
+            def _(side=side):
+                for number in numbers:
+                    edge(number, side).start()
+
+    send_edges((0, 1))
+
+    mobile_copy.wait()
+
+    send_edges((2,))
+
+    wait_start(1)
+
+    send_start(deferred)
+
+    for side in range(2):
+        @pl.when((has_low, has_high)[side])
+        def _(side=side):
+            for number in range(3):
+                edge(number, side).wait_send()
+                edge(number, 1 - side).wait_recv()
 
     lane = lax.broadcasted_iota(jnp.int32, (ROWS, nx), 1)
     not_first, not_last = lane > 0, lane < nx - 1
 
-    def update(source, target, layer):
+    def update(source, target, layer, skip=0):
         for row in range(0, ny, ROWS):
             here = pl.ds(row, ROWS)
             center = source[layer, pl.ds(PAD + row, ROWS), :]
@@ -199,8 +244,11 @@
             growth = mobile[layer - 1, here, :] * (1.0 + 0.5 * jnp.tanh(center)) * driving
             growth = growth * (1.0 - jnp.tanh(progress))
             if target is not None:
-                around = source[layer - 1, pl.ds(PAD + row, ROWS), :] + source[layer + 1, pl.ds(PAD + row, ROWS), :]
-                around = around + (source[layer, pl.ds(PAD + row - 1, ROWS), :] + source[layer, pl.ds(PAD + row + 1, ROWS), :])
+                around = source[layer, pl.ds(PAD + row - 1, ROWS), :] + source[layer, pl.ds(PAD + row + 1, ROWS), :]
+                if skip != -1:
+                    around = around + source[layer - 1, pl.ds(PAD + row, ROWS), :]
+                if skip != 1:
+                    around = around + source[layer + 1, pl.ds(PAD + row, ROWS), :]
                 left = jnp.where(not_first, pltpu.roll(center, 1, 1), 0.0)
                 right = jnp.where(not_last, pltpu.roll(center, nx - 1, 1), 0.0)
                 around = around + (left + right)
@@ -215,24 +263,34 @@
             return carry
         lax.fori_loop(low, high, body, 0)
 
+    def add_halo(source, middle, target, outer, inner, step, chunk):
+        for row in range(chunk * part, (chunk + 1) * part, ROWS):
+            here = pl.ds(PAD + row, ROWS)
+            value = middle[inner, here, :] + diffusion_number * source[outer, here, :]
+            middle[inner, here, :] = value
+            target[inner + step, here, :] = target[inner + step, here, :] + diffusion_number * value
+
     def cycle(source, middle, target, parity, go):
         sweep(source, middle, 3, thick + 1)
-        wait_halo(source, parity, 0, 0)
-        update(source, middle, 2)
-        update(middle, target, 3)
-        send_halo(target, 1 - parity, 0, 1, go)
-        wait_halo(source, parity, 1, 0)
-        update(source, middle, thick + 1)
-        update(middle, target, thick)
-        send_halo(target, 1 - parity, 1, 1, go)
-        wait_halo(source, parity, 0, 1)
-        sweep(source, middle, 1, jnp.where(has_low, 2, 1))
-        update(middle, target, 2)
-        send_halo(target, 1 - parity, 0, 0, go)
-        wait_halo(source, parity, 1, 1)
-        sweep(source, middle, thick + 2, jnp.where(has_high, thick + 3, thick + 2))
-        update(middle, target, thick + 1)
-        send_halo(target, 1 - parity, 1, 0, go)
+        for inner, step in ((2, 1), (thick + 1, -1)):
+            update(source, middle, inner, -step)
+            update(middle, target, inner + step, -step)
+        for side, inner, step in ((0, 2, 1), (1, thick + 1, -1)):
+            for chunk in range(CHUNKS):
+                wait_halo(source, parity, side, 0, chunk)
+                add_halo(source, middle, target, inner - step, inner, step, chunk)
+                send_halo(target, 1 - parity, side, 1, chunk, go)
+        for side, inner, step in ((0, 2, 1), (1, thick + 1, -1)):
+            @pl.when((has_low, has_high)[side])
+            def _(inner=inner, step=step):
+                update(source, middle, inner - step, -step)
+            update(middle, target, inner, -step)
+            for chunk in range(CHUNKS):
+                @pl.when((has_low, has_high)[side])
+                def _(side=side, inner=inner, step=step, chunk=chunk):
+                    wait_halo(source, parity, side, 1, chunk)
+                    add_halo(source, middle, target, inner - 2 * step, inner - step, step, chunk)
+                send_halo(target, 1 - parity, side, 0, chunk, go)
         sweep(middle, target, 4, thick)
         sweep(middle, None, jnp.where(has_low, 1, 2), 2)
         sweep(middle, None, thick + 2, jnp.where(has_high, thick + 3, thick + 2))
@@ -295,11 +353,13 @@
     lax.fori_loop(0, depth, keep_fine, 0)
     map_copy.wait()
 
-    @pl.when(jnp.logical_not(last))
-    def _():
-        for field in range(3):
-            for chain in range(2):
-                start_copy(guess.at[chain, field], chain, field, t + 1).wait_send()
+    wait_sent(later)
+
+    @pl.when(first)
+    def _():
+        for field in range(3):
+            for piece in range(2):
+                first_copy(half, field, piece).wait_send()
 
     @pl.when(later)
     def _():
@@ -374,8 +434,8 @@
         scratch_shapes=[
             heat, heat, heat, wide, wide, wide, pltpu.VMEM((depth, ny, nx), jnp.float32),
             both, one, both, one, pltpu.VMEM(coarse_map.shape, jnp.float32),
-            dma((2, 3)), dma((2, 3)), dma((3,)), dma, dma,
-            dma((2, 2, 2)), dma((2, 2, 2)), dma((3, 2)), dma((3, 2)),
+            dma((2, 3, 2)), dma((2, 3, 2)), dma((3,)), dma((3, 2)), dma, dma,
+            dma((2, 2, 2, CHUNKS)), dma((2, 2, 2, CHUNKS)), dma((3, 2)), dma((3, 2)),
             dma, dma, dma((3, depth)), dma((3, depth)), dma((depth,)), dma((depth,)), dma,
         ],
         compiler_params=pltpu.CompilerParams(

time: 127 us -> 116 us (0.913); the launches traced: 126 us -> 116 us
  Pallas kernels: 123 us -> 113 us
    pallas_call x1, Pallas kernels: 123 us -> 113 us  [shards(): pl.pallas_call(functools.partial(kernel, spaces, blocks), out_shape=jax.S...]
where the time goes in v1:
time: 116 us
  Pallas kernels  113 us (97%)
  local copies, waits for them, and re-layouts  2.7 us (2%)
    pallas_call x1, Pallas kernels, shards(): pl.pallas_call(functools.partial(kernel, spaces, blocks), out_shape=jax.S...  113 us
    unnamed x1, local copies, waits for them, and re-layouts  2.7 us

profile of v1, /device:TPU:15, one launch (start us, length us, event | category | flops | bytes accessed | tf_op | source)
XLA Modules:
  0.0 115.8 jit_solution(11436573946965337461)
XLA Ops:
  0.0 113.1 %shard_map.55 = f32[2,3,4,128,128]{4,3,2,1,0:T(8,128)} custom-call(f32[3,4,128,128]{3,2,1,0:T(8,128)} %initial.1, f32[2,3,4,128,128]{4,3,2,1,0:T(8,128)} %guess.1, f32[3,3,4,128,128]{4,3,2,1,0:T(8,128)} %coarse.1, s32[4,128,128]{2,1,0:T(8,128)} %sites.1, f32[1,128]{1,0:T(1,128)} %bitcast.1), custom_call_target="tpu_custom_call" | custom-call | tf_op jit(solution)/shard_map/pallas_call | solution.py:429
  113.1 2.7 %copy.7 = f32[2,3,4,128,128]{4,3,2,1,0:T(8,128)} copy(f32[2,3,4,128,128]{4,3,2,1,0:T(8,128)} %shard_map.55) | data formatting | bytes 3145728

commit v2 on v1

--- a/solution.py
+++ b/solution.py
@@ -11,7 +11,7 @@
 PAD = 8
 ROWS = 32
 EDGE = 2
-CHUNKS = 2
+CHUNKS = 4
 MESH = pl.DeviceIdType.MESH
 
 diffusion_number = 0.15
@@ -63,6 +63,12 @@
         (has_low, s - stride, t), (has_high, s + stride, t),
     ]
     count = 0
+    for there, layer in ((has_low, 0), (has_high, thick + 1)):
+        @pl.when(jnp.logical_not(there))
+        def _(layer=layer):
+            for ref in (dens, prog, mobile):
+                ref[layer] = jnp.zeros((ny, nx), jnp.float32)
+
     for there, space, tm in friends:
         @pl.when(there)
         def _(space=space, tm=tm):
@@ -114,14 +120,25 @@
         return carry
 
     lax.fori_loop(0, depth, look_up, 0)
-    mobile_copy = pltpu.make_async_remote_copy(
-        own_mobile, mobile.at[pl.ds(1 + half * depth, depth)], mob_send, mob_recv,
-        device_id=place(partner, t), device_id_type=MESH)
+    quarter = depth // 2
+    share = lax.rem(t, 2)
+
+    def mobile_copy():
+        return pltpu.make_async_remote_copy(
+            own_mobile.at[pl.ds(share * quarter, quarter)],
+            mobile.at[pl.ds(1 + half * depth + share * quarter, quarter)], mob_send.at[0], mob_recv.at[0],
+            device_id=place(partner, t), device_id_type=MESH)
+
+    def mobile_pass(which):
+        some = mobile.at[pl.ds(1 + other * depth + which * quarter, quarter)]
+        return pltpu.make_async_remote_copy(
+            some, some, mob_send.at[1], mob_recv.at[1],
+            device_id=place(s, t + 1 - 2 * share), device_id_type=MESH)
+
     pl.semaphore_wait(barrier, count)
 
     odd = lax.rem(t, 2) == 1
     deferred = jnp.logical_and(later, jnp.logical_not(odd))
-    mobile_late = jnp.logical_or(first, jnp.logical_and(odd, t > 2))
 
     def send_start(go):
         @pl.when(jnp.logical_and(jnp.logical_not(last), go))
@@ -131,12 +148,12 @@
                     for chain in range(2):
                         start_copy(half, chain, field, piece, t + 1).start()
 
-    def wait_sent(go):
+    def wait_sent(pieces, go):
         @pl.when(jnp.logical_and(jnp.logical_not(last), go))
         def _():
             for field in range(3):
                 for chain in range(2):
-                    for piece in range(2):
+                    for piece in pieces:
                         start_copy(half, chain, field, piece, t + 1).wait_send()
 
     def wait_start(piece):
@@ -150,12 +167,9 @@
 
     send_start(jnp.logical_not(deferred))
 
-    @pl.when(jnp.logical_not(mobile_late))
-    def _():
-        mobile_copy.start()
-
+    mobile_copy().start()
     map_copy.start()
-    wait_sent(first)
+    wait_sent((0,), first)
 
     @pl.when(first)
     def _():
@@ -166,10 +180,6 @@
             local_copy(field).wait()
 
     wait_start(0)
-
-    @pl.when(mobile_late)
-    def _():
-        mobile_copy.start()
 
     part = ny // CHUNKS
 
@@ -214,14 +224,15 @@
                     edge(number, side).start()
 
     send_edges((0, 1))
-
-    mobile_copy.wait()
+    send_start(deferred)
+
+    mobile_copy().wait()
+    mobile_pass(share).start()
+    mobile_pass(1 - share).wait_recv()
 
     send_edges((2,))
 
     wait_start(1)
-
-    send_start(deferred)
 
     for side in range(2):
         @pl.when((has_low, has_high)[side])
@@ -257,12 +268,6 @@
             dens[layer - 1, here, :] = density * ((1.0 - hardening) - growth) + hardening * saturation
             prog[layer - 1, here, :] = progress + growth
 
-    def sweep(source, target, low, high):
-        def body(layer, carry):
-            update(source, target, layer)
-            return carry
-        lax.fori_loop(low, high, body, 0)
-
     def add_halo(source, middle, target, outer, inner, step, chunk):
         for row in range(chunk * part, (chunk + 1) * part, ROWS):
             here = pl.ds(PAD + row, ROWS)
@@ -270,20 +275,40 @@
             middle[inner, here, :] = value
             target[inner + step, here, :] = target[inner + step, here, :] + diffusion_number * value
 
-    def cycle(source, middle, target, parity, go):
-        sweep(source, middle, 3, thick + 1)
-        for inner, step in ((2, 1), (thick + 1, -1)):
+    ends = ((0, 2, 1), (1, thick + 1, -1))
+
+    def fine_copy(field, chain, where, layer):
+        start = where * depth + layer
+        source = heat_a.at[start + 2, rows, :] if field == 0 else (dens, prog)[field - 1].at[start + 1]
+        return pltpu.make_async_remote_copy(
+            source, fine.at[chain, field, layer], back_send.at[field, layer], back_recv.at[field, layer],
+            device_id=place(partner, t), device_id_type=MESH)
+
+    def send_fine(piece):
+        low, layers = piece_of(other, piece)
+        for layer in range(layers):
+            for field in range(3):
+                fine_copy(field, half, other, low + layer).start()
+
+    def cycle(source, middle, target, parity, order, go):
+        for layer in range(3, thick + 1):
+            update(source, middle, layer)
+        for _, inner, step in order:
             update(source, middle, inner, -step)
+        for layer in range(4, thick):
+            update(middle, target, layer)
+        for _, inner, step in order:
             update(middle, target, inner + step, -step)
-        for side, inner, step in ((0, 2, 1), (1, thick + 1, -1)):
+        if go is not True:
+            @pl.when(jnp.logical_and(jnp.logical_not(go), later))
+            def _():
+                send_fine(1)
+        for side, inner, step in order:
             for chunk in range(CHUNKS):
                 wait_halo(source, parity, side, 0, chunk)
                 add_halo(source, middle, target, inner - step, inner, step, chunk)
                 send_halo(target, 1 - parity, side, 1, chunk, go)
-        for side, inner, step in ((0, 2, 1), (1, thick + 1, -1)):
-            @pl.when((has_low, has_high)[side])
-            def _(inner=inner, step=step):
-                update(source, middle, inner - step, -step)
+            update(source, middle, inner - step, -step)
             update(middle, target, inner, -step)
             for chunk in range(CHUNKS):
                 @pl.when((has_low, has_high)[side])
@@ -291,18 +316,10 @@
                     wait_halo(source, parity, side, 1, chunk)
                     add_halo(source, middle, target, inner - 2 * step, inner - step, step, chunk)
                 send_halo(target, 1 - parity, side, 0, chunk, go)
-        sweep(middle, target, 4, thick)
-        sweep(middle, None, jnp.where(has_low, 1, 2), 2)
-        sweep(middle, None, thick + 2, jnp.where(has_high, thick + 3, thick + 2))
+        for _, inner, step in order:
+            update(middle, None, inner - step)
 
     total = 2 * M // 4
-
-    def four_steps(index, carry):
-        cycle(heat_a, heat_b, heat_c, 0, True)
-        cycle(heat_c, heat_b, heat_a, 1, index < total - 1)
-        return carry
-
-    lax.fori_loop(0, total // 2, four_steps, 0)
 
     def state(field, layer):
         if field == 0:
@@ -319,31 +336,29 @@
                 relaxed_out[field, layer] = state(field, other * depth + layer)
         return carry
 
-    lax.fori_loop(0, depth, keep, 0)
-
     def relaxed_copy(chain):
         return pltpu.make_async_remote_copy(
             relaxed_out, relaxed.at[chain], relaxed_send, relaxed_recv,
             device_id=place(partner, t), device_id_type=MESH)
 
-    def fine_copy(field, chain, where, layer):
-        start = where * depth + layer
-        source = heat_a.at[start + 2, rows, :] if field == 0 else (dens, prog)[field - 1].at[start + 1]
-        return pltpu.make_async_remote_copy(
-            source, fine.at[chain, field, layer], back_send.at[field, layer], back_recv.at[field, layer],
-            device_id=place(partner, t), device_id_type=MESH)
+    def four_steps(index, carry):
+        @pl.when(index == total // 2)
+        def _():
+            lax.fori_loop(0, depth, keep, 0)
+
+            @pl.when(later)
+            def _():
+                relaxed_copy(half).start()
+
+        cycle(heat_a, heat_b, heat_c, 0, ends, True)
+        cycle(heat_c, heat_b, heat_a, 1, ends[::-1], index < total - 1)
+        return carry
+
+    lax.fori_loop(0, total, four_steps, 0)
 
     @pl.when(later)
     def _():
-        relaxed_copy(half).start()
-
-    lax.fori_loop(total // 2, total, four_steps, 0)
-
-    @pl.when(later)
-    def _():
-        for layer in range(depth):
-            for field in range(3):
-                fine_copy(field, half, other, layer).start()
+        send_fine(0)
 
     def keep_fine(layer, carry):
         for field in range(3):
@@ -353,7 +368,9 @@
     lax.fori_loop(0, depth, keep_fine, 0)
     map_copy.wait()
 
-    wait_sent(later)
+    wait_sent((0,), later)
+    wait_sent((1,), True)
+    mobile_pass(share).wait_send()
 
     @pl.when(first)
     def _():
@@ -371,7 +388,9 @@
             out.at[1, :, layer], arriving.at[:, layer], chain_send.at[layer], chain_recv.at[layer],
             device_id=place(s, tm), device_id_type=MESH)
 
-    def link(layer, carry):
+    def link(index, carry):
+        layer = lax.rem(index + other * EDGE, depth)
+
         @pl.when(first)
         def _():
             for field in range(3):
@@ -434,7 +453,7 @@
         scratch_shapes=[
             heat, heat, heat, wide, wide, wide, pltpu.VMEM((depth, ny, nx), jnp.float32),
             both, one, both, one, pltpu.VMEM(coarse_map.shape, jnp.float32),
-            dma((2, 3, 2)), dma((2, 3, 2)), dma((3,)), dma((3, 2)), dma, dma,
+            dma((2, 3, 2)), dma((2, 3, 2)), dma((3,)), dma((3, 2)), dma((2,)), dma((2,)),
             dma((2, 2, 2, CHUNKS)), dma((2, 2, 2, CHUNKS)), dma((3, 2)), dma((3, 2)),
             dma, dma, dma((3, depth)), dma((3, depth)), dma((depth,)), dma((depth,)), dma,
         ],

time: 116 us -> 111 us (0.957)
  Pallas kernels: 113 us -> 109 us
    pallas_call x1, Pallas kernels: 113 us -> 109 us  [shards(): pl.pallas_call(functools.partial(kernel, spaces, blocks), out_shape=jax.S...]
where the time goes in v2:
time: 111 us
  Pallas kernels  109 us (98%)
  local copies, waits for them, and re-layouts  2.7 us (2%)
    pallas_call x1, Pallas kernels, shards(): pl.pallas_call(functools.partial(kernel, spaces, blocks), out_shape=jax.S...  109 us
    unnamed x1, local copies, waits for them, and re-layouts  2.7 us

profile of v2, /device:TPU:15, one launch (start us, length us, event | category | flops | bytes accessed | tf_op | source)
XLA Modules:
  0.0 111.3 jit_solution(17991561147885674606)
XLA Ops:
  0.0 108.6 %shard_map.55 = f32[2,3,4,128,128]{4,3,2,1,0:T(8,128)} custom-call(f32[3,4,128,128]{3,2,1,0:T(8,128)} %initial.1, f32[2,3,4,128,128]{4,3,2,1,0:T(8,128)} %guess.1, f32[3,3,4,128,128]{4,3,2,1,0:T(8,128)} %coarse.1, s32[4,128,128]{2,1,0:T(8,128)} %sites.1, f32[1,128]{1,0:T(1,128)} %bitcast.1), custom_call_target="tpu_custom_call" | custom-call | tf_op jit(solution)/shard_map/pallas_call | solution.py:448
  108.6 2.7 %copy.7 = f32[2,3,4,128,128]{4,3,2,1,0:T(8,128)} copy(f32[2,3,4,128,128]{4,3,2,1,0:T(8,128)} %shard_map.55) | data formatting | bytes 3145728

commit v3 on v2

--- a/solution.py
+++ b/solution.py
@@ -35,6 +35,14 @@
     half = lax.rem(s, 2)
     first, last = t == 0, t == blocks - 1
     later = jnp.logical_not(first)
+    share = lax.rem(t, 2)
+    odd = share == 1
+    mate = t + 1 - 2 * share
+    opening = t == 1
+    distant = jnp.logical_and(odd, t > 2)
+    near = jnp.logical_not(distant)
+    sender = jnp.logical_and(odd, t + 2 < blocks)
+    both_ways = jnp.logical_not(opening)
     thick, stride = 2 * depth, 2
     offset = half * depth
     other = 1 - half
@@ -57,9 +65,11 @@
             heat[layer, rows, :] = jnp.zeros((ny, nx), jnp.float32)
 
     friends = [
-        (t >= 0, partner, t),
-        (t > 0, base, t - 1), (t > 0, base + 1, t - 1),
-        (t < blocks - 1, base, t + 1), (t < blocks - 1, base + 1, t + 1),
+        (t >= 0, partner, t), (t >= 0, s, mate), (t >= 0, partner, mate),
+        (distant, base, t - 2), (distant, base + 1, t - 2),
+        (sender, base, t + 2), (sender, base + 1, t + 2),
+        (jnp.logical_and(odd, t + 1 < blocks), s, t + 1),
+        (jnp.logical_and(jnp.logical_not(odd), t > 0), s, t - 1),
         (has_low, s - stride, t), (has_high, s + stride, t),
     ]
     count = 0
@@ -74,6 +84,7 @@
         def _(space=space, tm=tm):
             pl.semaphore_signal(barrier, 1, device_id=place(space, tm), device_id_type=MESH)
         count = count + there.astype(jnp.int32)
+
     def piece_of(source, piece):
         if piece == 0:
             return source * (depth - EDGE), EDGE
@@ -92,22 +103,37 @@
             start_send.at[chain, field, piece], start_recv.at[source, field, piece],
             device_id=place(base + chain, tm), device_id_type=MESH)
 
-    def local_copy(field):
-        return pltpu.make_async_copy(initial.at[field], landing(field, half, 0, depth), local_sem.at[field])
-
-    def first_copy(source, field, piece):
-        low, layers = piece_of(source, piece)
-        return pltpu.make_async_remote_copy(
-            initial.at[field, pl.ds(low, layers)], landing(field, source, low, layers),
-            first_send.at[field, piece], start_recv.at[source, field, piece],
+    def own_start(field, low, layers, mine):
+        some = pl.ds(low, layers)
+        return guess.at[half if mine else other, field, some], initial.at[field, some]
+
+    def local_copy(field, source):
+        return pltpu.make_async_copy(
+            own_start(field, 0, depth, True)[source], landing(field, half, 0, depth), local_sem.at[field])
+
+    def swap_copy(field, piece, source):
+        low, layers = piece_of(half, piece)
+        return pltpu.make_async_remote_copy(
+            own_start(field, low, layers, False)[source], landing(field, half, low, layers),
+            first_send.at[field, piece], start_recv.at[half, field, piece],
             device_id=place(partner, t), device_id_type=MESH)
 
+    def send_swap(source):
+        for piece in range(2):
+            for field in range(3):
+                swap_copy(field, piece, source).start()
+
     map_copy = pltpu.make_async_copy(coarse, maps, map_sem)
 
-    @pl.when(first)
-    def _():
-        for field in range(3):
-            local_copy(field).start()
+    @pl.when(jnp.logical_not(odd))
+    def _():
+        for field in range(3):
+            local_copy(field, 0).start()
+
+    @pl.when(opening)
+    def _():
+        for field in range(3):
+            local_copy(field, 1).start()
 
     table = jnp.broadcast_to(mobility[...], (8, nx))
 
@@ -121,7 +147,6 @@
 
     lax.fori_loop(0, depth, look_up, 0)
     quarter = depth // 2
-    share = lax.rem(t, 2)
 
     def mobile_copy():
         return pltpu.make_async_remote_copy(
@@ -133,51 +158,53 @@
         some = mobile.at[pl.ds(1 + other * depth + which * quarter, quarter)]
         return pltpu.make_async_remote_copy(
             some, some, mob_send.at[1], mob_recv.at[1],
-            device_id=place(s, t + 1 - 2 * share), device_id_type=MESH)
+            device_id=place(s, mate), device_id_type=MESH)
 
     pl.semaphore_wait(barrier, count)
 
-    odd = lax.rem(t, 2) == 1
-    deferred = jnp.logical_and(later, jnp.logical_not(odd))
-
-    def send_start(go):
-        @pl.when(jnp.logical_and(jnp.logical_not(last), go))
-        def _():
-            for piece in range(2):
-                for field in range(3):
-                    for chain in range(2):
-                        start_copy(half, chain, field, piece, t + 1).start()
-
-    def wait_sent(pieces, go):
-        @pl.when(jnp.logical_and(jnp.logical_not(last), go))
+    def wait_sent(pieces):
+        @pl.when(sender)
         def _():
             for field in range(3):
                 for chain in range(2):
                     for piece in pieces:
-                        start_copy(half, chain, field, piece, t + 1).wait_send()
+                        start_copy(half, chain, field, piece, t + 2).wait_send()
 
     def wait_start(piece):
         for field in range(3):
             start_copy(other, 0, field, piece, t).wait_recv()
 
-        @pl.when(later)
+        @pl.when(distant)
         def _():
             for field in range(3):
                 start_copy(half, 0, field, piece, t).wait_recv()
 
-    send_start(jnp.logical_not(deferred))
-
     mobile_copy().start()
+
+    @pl.when(jnp.logical_not(odd))
+    def _():
+        send_swap(0)
+
+    @pl.when(sender)
+    def _():
+        for piece in range(2):
+            for field in range(3):
+                for chain in range(2):
+                    start_copy(half, chain, field, piece, t + 2).start()
+
+    mobile_copy().wait()
+    mobile_pass(share).start()
     map_copy.start()
-    wait_sent((0,), first)
-
-    @pl.when(first)
-    def _():
-        for piece in range(2):
-            for field in range(3):
-                first_copy(half, field, piece).start()
-        for field in range(3):
-            local_copy(field).wait()
+    wait_sent((0,))
+
+    @pl.when(opening)
+    def _():
+        send_swap(1)
+
+    @pl.when(near)
+    def _():
+        for field in range(3):
+            local_copy(field, 0).wait()
 
     wait_start(0)
 
@@ -224,10 +251,7 @@
                     edge(number, side).start()
 
     send_edges((0, 1))
-    send_start(deferred)
-
-    mobile_copy().wait()
-    mobile_pass(share).start()
+
     mobile_pass(1 - share).wait_recv()
 
     send_edges((2,))
@@ -277,18 +301,24 @@
 
     ends = ((0, 2, 1), (1, thick + 1, -1))
 
-    def fine_copy(field, chain, where, layer):
+    def fine_copy(field, where, layer, slot):
         start = where * depth + layer
         source = heat_a.at[start + 2, rows, :] if field == 0 else (dens, prog)[field - 1].at[start + 1]
         return pltpu.make_async_remote_copy(
-            source, fine.at[chain, field, layer], back_send.at[field, layer], back_recv.at[field, layer],
-            device_id=place(partner, t), device_id_type=MESH)
+            source, fine.at[slot, field, layer], back_send.at[where, field, layer], back_recv.at[slot, field, layer],
+            device_id=place(base + where, mate), device_id_type=MESH)
 
     def send_fine(piece):
-        low, layers = piece_of(other, piece)
-        for layer in range(layers):
-            for field in range(3):
-                fine_copy(field, half, other, low + layer).start()
+        def send(where):
+            low, layers = piece_of(where, piece)
+            for layer in range(layers):
+                for field in range(3):
+                    fine_copy(field, where, low + layer, half).start()
+
+        @pl.when(both_ways)
+        def _():
+            send(other)
+        send(half)
 
     def cycle(source, middle, target, parity, order, go):
         for layer in range(3, thick + 1):
@@ -300,7 +330,7 @@
         for _, inner, step in order:
             update(middle, target, inner + step, -step)
         if go is not True:
-            @pl.when(jnp.logical_and(jnp.logical_not(go), later))
+            @pl.when(jnp.logical_not(go))
             def _():
                 send_fine(1)
         for side, inner, step in order:
@@ -327,28 +357,25 @@
         return (dens, prog)[field - 1][layer + 1]
 
     def keep(layer, carry):
-        for field in range(3):
-            relaxed[half, field, layer] = state(field, offset + layer)
-
-        @pl.when(later)
-        def _():
-            for field in range(3):
-                relaxed_out[field, layer] = state(field, other * depth + layer)
+        for where in range(2):
+            for field in range(3):
+                relaxed_out[where, field, layer] = state(field, where * depth + layer)
         return carry
 
-    def relaxed_copy(chain):
-        return pltpu.make_async_remote_copy(
-            relaxed_out, relaxed.at[chain], relaxed_send, relaxed_recv,
-            device_id=place(partner, t), device_id_type=MESH)
+    def relaxed_copy(where, slot):
+        return pltpu.make_async_remote_copy(
+            relaxed_out.at[where], relaxed.at[slot], relaxed_send.at[where], relaxed_recv.at[slot],
+            device_id=place(base + where, mate), device_id_type=MESH)
 
     def four_steps(index, carry):
         @pl.when(index == total // 2)
         def _():
             lax.fori_loop(0, depth, keep, 0)
-
-            @pl.when(later)
+            relaxed_copy(half, half).start()
+
+            @pl.when(both_ways)
             def _():
-                relaxed_copy(half).start()
+                relaxed_copy(other, half).start()
 
         cycle(heat_a, heat_b, heat_c, 0, ends, True)
         cycle(heat_c, heat_b, heat_a, 1, ends[::-1], index < total - 1)
@@ -356,32 +383,28 @@
 
     lax.fori_loop(0, total, four_steps, 0)
 
+    send_fine(0)
+    map_copy.wait()
+    wait_sent((1,))
+    mobile_pass(share).wait_send()
+
+    @pl.when(near)
+    def _():
+        for field in range(3):
+            for piece in range(2):
+                swap_copy(field, piece, 0).wait_send()
+
+    relaxed_copy(half, half).wait_send()
+
+    @pl.when(both_ways)
+    def _():
+        relaxed_copy(other, half).wait_send()
+
+    relaxed_copy(half, half).wait_recv()
+
     @pl.when(later)
     def _():
-        send_fine(0)
-
-    def keep_fine(layer, carry):
-        for field in range(3):
-            fine[half, field, layer] = state(field, offset + layer)
-        return carry
-
-    lax.fori_loop(0, depth, keep_fine, 0)
-    map_copy.wait()
-
-    wait_sent((0,), later)
-    wait_sent((1,), True)
-    mobile_pass(share).wait_send()
-
-    @pl.when(first)
-    def _():
-        for field in range(3):
-            for piece in range(2):
-                first_copy(half, field, piece).wait_send()
-
-    @pl.when(later)
-    def _():
-        relaxed_copy(half).wait_send()
-        relaxed_copy(other).wait_recv()
+        relaxed_copy(half, other).wait_recv()
 
     def chain_copy(layer, tm):
         return pltpu.make_async_remote_copy(
@@ -391,6 +414,9 @@
     def link(index, carry):
         layer = lax.rem(index + other * EDGE, depth)
 
+        for field in range(3):
+            fine_copy(field, half, layer, half).wait_recv()
+
         @pl.when(first)
         def _():
             for field in range(3):
@@ -400,7 +426,7 @@
         @pl.when(later)
         def _():
             for field in range(3):
-                fine_copy(field, other, half, layer).wait_recv()
+                fine_copy(field, half, layer, other).wait_recv()
             chain_copy(layer, t).wait_recv()
             for row in range(0, ny, ROWS):
                 here = pl.ds(row, ROWS)
@@ -428,11 +454,15 @@
         for layer in range(depth):
             chain_copy(layer, t + 1).wait_send()
 
-    @pl.when(later)
+    for layer in range(depth):
+        for field in range(3):
+            fine_copy(field, half, layer, half).wait_send()
+
+    @pl.when(both_ways)
     def _():
         for layer in range(depth):
             for field in range(3):
-                fine_copy(field, half, other, layer).wait_send()
+                fine_copy(field, other, layer, half).wait_send()
 
 
 def shards(spaces, blocks, initial, guess, coarse_map, sites, mobility):
@@ -452,10 +482,10 @@
         out_specs=vmem,
         scratch_shapes=[
             heat, heat, heat, wide, wide, wide, pltpu.VMEM((depth, ny, nx), jnp.float32),
-            both, one, both, one, pltpu.VMEM(coarse_map.shape, jnp.float32),
+            both, both, both, one, pltpu.VMEM(coarse_map.shape, jnp.float32),
             dma((2, 3, 2)), dma((2, 3, 2)), dma((3,)), dma((3, 2)), dma((2,)), dma((2,)),
             dma((2, 2, 2, CHUNKS)), dma((2, 2, 2, CHUNKS)), dma((3, 2)), dma((3, 2)),
-            dma, dma, dma((3, depth)), dma((3, depth)), dma((depth,)), dma((depth,)), dma,
+            dma((2,)), dma((2,)), dma((2, 3, depth)), dma((2, 3, depth)), dma((depth,)), dma((depth,)), dma,
         ],
         compiler_params=pltpu.CompilerParams(
             collective_id=0, has_side_effects=True, vmem_limit_bytes=60 * 1024 * 1024),

time: 111 us -> 104 us (0.937); the launches traced: 111 us -> 103 us
  Pallas kernels: 109 us -> 100 us
    pallas_call x1, Pallas kernels: 109 us -> 100 us  [shards(): pl.pallas_call(functools.partial(kernel, spaces, blocks), out_shape=jax.S...]
where the time goes in v3:
time: 104 us; the launch traced here: 103 us
  Pallas kernels  100 us (96%)
  local copies, waits for them, and re-layouts  2.7 us (3%)
    pallas_call x1, Pallas kernels, shards(): pl.pallas_call(functools.partial(kernel, spaces, blocks), out_shape=jax.S...  100 us
    unnamed x1, local copies, waits for them, and re-layouts  2.7 us

profile of v3, /device:TPU:15, one launch (start us, length us, event | category | flops | bytes accessed | tf_op | source)
XLA Modules:
  0.0 102.9 jit_solution(5572706057809661503)
XLA Ops:
  0.0 100.2 %shard_map.55 = f32[2,3,4,128,128]{4,3,2,1,0:T(8,128)} custom-call(f32[3,4,128,128]{3,2,1,0:T(8,128)} %initial.1, f32[2,3,4,128,128]{4,3,2,1,0:T(8,128)} %guess.1, f32[3,3,4,128,128]{4,3,2,1,0:T(8,128)} %coarse.1, s32[4,128,128]{2,1,0:T(8,128)} %sites.1, f32[1,128]{1,0:T(1,128)} %bitcast.1), custom_call_target="tpu_custom_call" | custom-call | tf_op jit(solution)/shard_map/pallas_call | solution.py:478
  100.2 2.7 %copy.7 = f32[2,3,4,128,128]{4,3,2,1,0:T(8,128)} copy(f32[2,3,4,128,128]{4,3,2,1,0:T(8,128)} %shard_map.55) | data formatting | bytes 3145728

commit v4 on v3

--- a/solution.py
+++ b/solution.py
@@ -11,7 +11,9 @@
 PAD = 8
 ROWS = 32
 EDGE = 2
-CHUNKS = 4
+CHUNKS = 8
+SOME = 16
+PARTS = 2
 MESH = pl.DeviceIdType.MESH
 
 diffusion_number = 0.15
@@ -22,12 +24,12 @@
 
 def kernel(
     spaces, blocks,
-    initial, guess, coarse, sites, mobility, out,
+    initial, guess, coarse, sites, mobility, result,
     heat_a, heat_b, heat_c, dens, prog, mobile, own_mobile,
-    relaxed, relaxed_out, fine, arriving, maps,
+    relaxed, relaxed_out, fine, out, arriving, maps,
     start_send, start_recv, local_sem, first_send, mob_send, mob_recv,
     halo_send, halo_recv, edge_send, edge_recv,
-    relaxed_send, relaxed_recv, back_send, back_recv, chain_send, chain_recv, map_sem,
+    relaxed_send, relaxed_recv, back_send, back_recv, chain_send, chain_recv, map_sem, out_sem,
 ):
     depth = sites.shape[0]
     ny, nx = sites.shape[1], sites.shape[2]
@@ -293,8 +295,8 @@
             prog[layer - 1, here, :] = progress + growth
 
     def add_halo(source, middle, target, outer, inner, step, chunk):
-        for row in range(chunk * part, (chunk + 1) * part, ROWS):
-            here = pl.ds(PAD + row, ROWS)
+        for row in range(chunk * part, (chunk + 1) * part, SOME):
+            here = pl.ds(PAD + row, SOME)
             value = middle[inner, here, :] + diffusion_number * source[outer, here, :]
             middle[inner, here, :] = value
             target[inner + step, here, :] = target[inner + step, here, :] + diffusion_number * value
@@ -308,17 +310,11 @@
             source, fine.at[slot, field, layer], back_send.at[where, field, layer], back_recv.at[slot, field, layer],
             device_id=place(base + where, mate), device_id_type=MESH)
 
-    def send_fine(piece):
-        def send(where):
-            low, layers = piece_of(where, piece)
-            for layer in range(layers):
-                for field in range(3):
-                    fine_copy(field, where, low + layer, half).start()
-
-        @pl.when(both_ways)
-        def _():
-            send(other)
-        send(half)
+    def send_fine(where, piece):
+        low, layers = piece_of(where, piece)
+        for layer in range(layers):
+            for field in range(3):
+                fine_copy(field, where, low + layer, half).start()
 
     def cycle(source, middle, target, parity, order, go):
         for layer in range(3, thick + 1):
@@ -330,9 +326,13 @@
         for _, inner, step in order:
             update(middle, target, inner + step, -step)
         if go is not True:
+            @pl.when(jnp.logical_and(jnp.logical_not(go), both_ways))
+            def _():
+                send_fine(other, 1)
+
             @pl.when(jnp.logical_not(go))
             def _():
-                send_fine(1)
+                send_fine(half, 1)
         for side, inner, step in order:
             for chunk in range(CHUNKS):
                 wait_halo(source, parity, side, 0, chunk)
@@ -346,6 +346,12 @@
                     wait_halo(source, parity, side, 1, chunk)
                     add_halo(source, middle, target, inner - 2 * step, inner - step, step, chunk)
                 send_halo(target, 1 - parity, side, 0, chunk, go)
+            if go is not True:
+                mine = jnp.logical_or(both_ways, half == side)
+
+                @pl.when(jnp.logical_and(jnp.logical_not(go), mine))
+                def _(side=side):
+                    send_fine(side, 0)
         for _, inner, step in order:
             update(middle, None, inner - step)
 
@@ -378,12 +384,11 @@
                 relaxed_copy(other, half).start()
 
         cycle(heat_a, heat_b, heat_c, 0, ends, True)
-        cycle(heat_c, heat_b, heat_a, 1, ends[::-1], index < total - 1)
+        cycle(heat_c, heat_b, heat_a, 1, ends, index < total - 1)
         return carry
 
     lax.fori_loop(0, total, four_steps, 0)
 
-    send_fine(0)
     map_copy.wait()
     wait_sent((1,))
     mobile_pass(share).wait_send()
@@ -406,14 +411,20 @@
     def _():
         relaxed_copy(half, other).wait_recv()
 
-    def chain_copy(layer, tm):
-        return pltpu.make_async_remote_copy(
-            out.at[1, :, layer], arriving.at[:, layer], chain_send.at[layer], chain_recv.at[layer],
+    slab = ny // PARTS
+
+    def chain_copy(layer, piece, tm):
+        some = pl.ds(piece * slab, slab)
+        return pltpu.make_async_remote_copy(
+            out.at[1, :, layer, some, :], arriving.at[:, layer, some, :],
+            chain_send.at[layer, piece], chain_recv.at[layer, piece],
             device_id=place(s, tm), device_id_type=MESH)
+
+    def result_copy(layer):
+        return pltpu.make_async_copy(out.at[:, :, layer], result.at[:, :, layer], out_sem.at[layer])
 
     def link(index, carry):
         layer = lax.rem(index + other * EDGE, depth)
-
         for field in range(3):
             fine_copy(field, half, layer, half).wait_recv()
 
@@ -422,37 +433,46 @@
             for field in range(3):
                 out[0, field, layer] = relaxed[half, field, layer]
                 out[1, field, layer] = fine[half, field, layer]
+            for piece in range(PARTS):
+                chain_copy(layer, piece, t + 1).start()
 
         @pl.when(later)
         def _():
             for field in range(3):
                 fine_copy(field, half, layer, other).wait_recv()
-            chain_copy(layer, t).wait_recv()
-            for row in range(0, ny, ROWS):
-                here = pl.ds(row, ROWS)
-                value = [arriving[field, layer, here, :] for field in range(3)]
-                for slot in range(2):
-                    change = [value[field] - relaxed[slot, field, layer, here, :] for field in range(3)]
-                    value = [
-                        fine[slot, r, layer, here, :]
-                        + (maps[r, 0, layer, here, :] * change[0] + maps[r, 1, layer, here, :] * change[1]
-                           + maps[r, 2, layer, here, :] * change[2])
-                        for r in range(3)
-                    ]
-                    for field in range(3):
-                        out[slot, field, layer, here, :] = value[field]
-
-        @pl.when(jnp.logical_not(last))
-        def _():
-            chain_copy(layer, t + 1).start()
+            for piece in range(PARTS):
+                chain_copy(layer, piece, t).wait_recv()
+                for row in range(piece * slab, (piece + 1) * slab, ROWS):
+                    here = pl.ds(row, ROWS)
+                    value = [arriving[field, layer, here, :] for field in range(3)]
+                    for slot in range(2):
+                        change = [value[field] - relaxed[slot, field, layer, here, :] for field in range(3)]
+                        value = [
+                            fine[slot, r, layer, here, :]
+                            + (maps[r, 0, layer, here, :] * change[0] + maps[r, 1, layer, here, :] * change[1]
+                               + maps[r, 2, layer, here, :] * change[2])
+                            for r in range(3)
+                        ]
+                        for field in range(3):
+                            out[slot, field, layer, here, :] = value[field]
+
+                @pl.when(jnp.logical_not(last))
+                def _(piece=piece):
+                    chain_copy(layer, piece, t + 1).start()
+
+        result_copy(layer).start()
         return carry
 
     lax.fori_loop(0, depth, link, 0)
 
+    for layer in range(depth):
+        result_copy(layer).wait()
+
     @pl.when(jnp.logical_not(last))
     def _():
         for layer in range(depth):
-            chain_copy(layer, t + 1).wait_send()
+            for piece in range(PARTS):
+                chain_copy(layer, piece, t + 1).wait_send()
 
     for layer in range(depth):
         for field in range(3):
@@ -479,13 +499,13 @@
         functools.partial(kernel, spaces, blocks),
         out_shape=jax.ShapeDtypeStruct(guess.shape, jnp.float32),
         in_specs=[hbm, hbm, hbm, vmem, vmem],
-        out_specs=vmem,
+        out_specs=hbm,
         scratch_shapes=[
             heat, heat, heat, wide, wide, wide, pltpu.VMEM((depth, ny, nx), jnp.float32),
-            both, both, both, one, pltpu.VMEM(coarse_map.shape, jnp.float32),
+            both, both, both, both, one, pltpu.VMEM(coarse_map.shape, jnp.float32),
             dma((2, 3, 2)), dma((2, 3, 2)), dma((3,)), dma((3, 2)), dma((2,)), dma((2,)),
             dma((2, 2, 2, CHUNKS)), dma((2, 2, 2, CHUNKS)), dma((3, 2)), dma((3, 2)),
-            dma((2,)), dma((2,)), dma((2, 3, depth)), dma((2, 3, depth)), dma((depth,)), dma((depth,)), dma,
+            dma((2,)), dma((2,)), dma((2, 3, depth)), dma((2, 3, depth)), dma((depth, PARTS)), dma((depth, PARTS)), dma, dma((depth,)),
         ],
         compiler_params=pltpu.CompilerParams(
             collective_id=0, has_side_effects=True, vmem_limit_bytes=60 * 1024 * 1024),

time: 104 us -> 103 us (level)
  no operation moved by 1% of the time
where the time goes in v4:
time: 103 us
  Pallas kernels  99.8 us (97%)
  local copies, waits for them, and re-layouts  2.7 us (3%)
    pallas_call x1, Pallas kernels, shards(): pl.pallas_call(functools.partial(kernel, spaces, blocks), out_shape=jax.S...  99.8 us
    unnamed x1, local copies, waits for them, and re-layouts  2.7 us

profile of v4, /device:TPU:15, one launch (start us, length us, event | category | flops | bytes accessed | tf_op | source)
XLA Modules:
  0.0 102.5 jit_solution(10294942990365857519)
XLA Ops:
  0.0 99.8 %shard_map.55 = f32[2,3,4,128,128]{4,3,2,1,0:T(8,128)} custom-call(f32[3,4,128,128]{3,2,1,0:T(8,128)} %initial.1, f32[2,3,4,128,128]{4,3,2,1,0:T(8,128)} %guess.1, f32[3,3,4,128,128]{4,3,2,1,0:T(8,128)} %coarse.1, s32[4,128,128]{2,1,0:T(8,128)} %sites.1, f32[1,128]{1,0:T(1,128)} %bitcast.1), custom_call_target="tpu_custom_call" | custom-call | tf_op jit(solution)/shard_map/pallas_call | solution.py:498
  99.8 2.7 %copy.7 = f32[2,3,4,128,128]{4,3,2,1,0:T(8,128)} copy(f32[2,3,4,128,128]{4,3,2,1,0:T(8,128)} %shard_map.55) | data formatting | bytes 3145728
